TPU v7x, 32 devices: a whole 2x2x4 slice. The times are simulated.
32 devices in a mesh: groups: 2 (over y), prow: 4 (over x, core), pcol: 4 (over z).
Axes of the slice: x: 2, y: 2, z: 4, core: 2. Of those that a mesh axis runs over, the one named last changes fastest.
Arguments:
- rhs: bfloat16 [8, 32, 2048], P('groups', None, 'pcol'), parts along dimension 0, may hold values from -6 to 6
- dinv: bfloat16 [8, 512, 2048], P('groups', None, 'pcol'), parts along dimension 0
- tiles: bfloat16 [128, 512, 512], P(('groups', 'prow', 'pcol')), parts along dimension 0, may hold values from -0.09375 to 0.09375
- tile_source: int32 [128], P(('groups', 'prow', 'pcol')), parts along dimension 0, may hold values from 0 to 11, as said below
- tile_target: int32 [128], P(('groups', 'prow', 'pcol')), parts along dimension 0, may hold values from -1 to 3, as said below
Outputs:
- solution: bfloat16 [8, 32, 2048], P('groups', None, 'pcol'), parts along dimension 0
There are 2 independent parts, one for each index of `groups`. A program takes and returns all parts, laid end to end along the dimension named above; each array names one. Nothing has to cross between parts.
Inputs may be any that keep to these rules, and one draw needn't show every extreme that they name: tile_source // 4 is smaller than tile_target in every filled slot. `tile_target`: -1 marks an empty slot; a grid position's filled slots come first; some positions fill all 4, others only one.
All inputs are finite; a program needn't handle non-finite values.
Results may differ from a plain program's by a relative error of at most 0.0055.
Values may be sent and summed in bfloat16 or wider, within the bound.
A program may use at most 64 MiB of HBM per device.

v0:
```python
import jax
import jax.numpy as jnp
from jax import lax
from jax.sharding import PartitionSpec as P


def apply_right(left, matrix):
    return lax.dot_general(
        left, matrix, (((1,), (1,)), ((), ())), preferred_element_type=jnp.float32
    )


def spread(partial_value, level, tiles, src_level, src_col, tile_target, pick):
    levels = partial_value.shape[0]
    empty = jnp.zeros(partial_value.shape[1:], jnp.float32)
    for slot in range(tiles.shape[0]):
        active = (src_level[slot] == level) & (tile_target[slot] > level)
        term = lax.cond(
            active, lambda slot=slot: apply_right(pick(src_col[slot]), tiles[slot]), lambda: empty
        )
        onehot = (jnp.arange(levels, dtype=jnp.int32) == tile_target[slot]).astype(jnp.float32)
        partial_value = partial_value + onehot[:, None, None] * term[None]
    return partial_value


def body(rhs, dinv, tiles, tile_source, tile_target):
    levels = rhs.shape[0]
    samples = rhs.shape[1]
    width = rhs.shape[2]
    columns = lax.axis_size("pcol")
    src_level = tile_source // columns
    src_col = tile_source % columns
    partial_value = jnp.zeros((levels, samples, width), jnp.float32)
    solved = []
    for level in range(levels):
        if level == 0:
            short = rhs[0].astype(jnp.float32)
        else:
            short = rhs[level].astype(jnp.float32) - lax.psum(partial_value[level], "prow")
        block = apply_right(short.astype(jnp.bfloat16), dinv[level]).astype(jnp.bfloat16)
        solved.append(block)
        if level + 1 < levels:
            gathered = lax.all_gather(block[None], "pcol", axis=0, tiled=True)

            def pick(col, gathered=gathered):
                return lax.dynamic_index_in_dim(gathered, col, 0, keepdims=False)

            partial_value = spread(
                partial_value, level, tiles, src_level, src_col, tile_target, pick
            )
    return jnp.stack(solved)


def solution(mesh):
    placed = (
        P("groups", None, "pcol"),
        P("groups", None, "pcol"),
        P(("groups", "prow", "pcol"), None, None),
        P(("groups", "prow", "pcol")),
        P(("groups", "prow", "pcol")),
    )
    return jax.shard_map(
        body, mesh=mesh, in_specs=placed, out_specs=P("groups", None, "pcol"), check_vma=False
    )
```

profile of v0, /device:TPU:0, one launch (start us, length us, event | category | flops | bytes accessed | tf_op | source)
XLA Modules:
  0.0 189.5 jit_solution(18130619797718618467)
XLA Ops:
  6.5 0.0 all-reduce.4.cloned.1.call-start
  6.5 1.5 fusion.99
  9.2 1.2 compare_convert_fusion.2
  11.7 1.2 compare_convert_fusion
  13.0 0.7 and_select_fusion
  13.6 0.6 fusion.100
  16.8 0.0 copy-start
  16.8 0.0 copy-start.1
  16.8 1.4 convolution_convert_fusion.3
  18.3 15.1 %all-gather = bf16[128,512]{1,0:T(8,128)(2,1)S(1)} all-gather(bf16[32,512]{1,0:T(8,128)(2,1)S(1)} %convolution_convert_fusion.3), channel_id=2, replica_groups=mesh['groups'=2,'prow'=4,'pcol'=4] {'pcol'}, dimensions={0}, use_global_device_ids=true | all-gather | bytes 163840 | tf_op jit(solution)/shard_map/all_gather | solution.py:43
  33.4 3.8 %conditional.13 = (f32[32,512]{1,0:T(8,128)S(1)}) conditional(s32[]{:T(128)} %convert_element_type.119, () %tuple.79, (s32[4]{0:T(128)S(1)}, bf16[4,32,512]{2,1,0:T(8,128)(2,1)S(1)}, bf16[4,512,512]{2,1,0:T(8,128)(2,1)}) %tuple.133), branch_computations={%region_2.3_spmd, %region_3.4_spmd} | conditional | flops 16777220 | bytes 622646 | solution.py:18
  33.4 0.6 slice.30
  35.9 1.3 fusion.6
  37.2 0.1 multiply_add_fusion.1
  37.4 0.6 slice_bitcast_fusion.1
  38.0 0.0 all-reduce.4.cloned.1.call-update
  38.0 0.0 all-reduce.6.cloned.1.call-start
  43.0 34.6 %all-reduce.4.cloned.1.call-done = f32[32,512]{1,0:T(8,128)} async-done(((f32[32,512]{1,0:T(8,128)}), f32[32,512]{1,0:T(8,128)}) %all-reduce.4.cloned.1.call-update) | async-done | bytes 65552 | tf_op jit(solution)/shard_map/psum | solution.py:39
  77.7 0.0 copy-done
  77.7 0.0 copy-done.1
  77.7 1.1 convolution_convert_fusion.2
  78.8 13.4 %all-gather.1 = bf16[128,512]{1,0:T(8,128)(2,1)S(1)} all-gather(bf16[32,512]{1,0:T(8,128)(2,1)S(1)} %convolution_convert_fusion.2), channel_id=3, replica_groups=mesh['groups'=2,'prow'=4,'pcol'=4] {'pcol'}, dimensions={0}, use_global_device_ids=true | all-gather | bytes 163840 | tf_op jit(solution)/shard_map/all_gather | solution.py:43
  92.2 3.8 %conditional.19 = (f32[32,512]{1,0:T(8,128)S(1)}) conditional(s32[]{:T(128)} %convert_element_type.131, () %tuple.86, (s32[4]{0:T(128)S(1)}, bf16[4,32,512]{2,1,0:T(8,128)(2,1)S(1)}, bf16[4,512,512]{2,1,0:T(8,128)(2,1)}) %tuple.139), branch_computations={%region_15.16_spmd, %region_16.17_spmd} | conditional | flops 16777220 | bytes 622646 | solution.py:18
  92.2 0.6 slice.53
  94.7 1.3 fusion.42
  96.1 0.2 multiply_add_fusion
  96.3 0.6 slice_bitcast_fusion
  96.9 0.0 all-reduce.6.cloned.1.call-update
  97.0 0.0 all-reduce.8.cloned.1.call-start
  102.0 0.6 slice.178
  102.5 0.6 slice.180
  103.2 0.6 slice.181
  103.8 0.6 slice.182
  104.4 24.2 %all-reduce.6.cloned.1.call-done = f32[32,512]{1,0:T(8,128)} async-done(((f32[32,512]{1,0:T(8,128)}), f32[32,512]{1,0:T(8,128)}) %all-reduce.6.cloned.1.call-update) | async-done | bytes 65552 | tf_op jit(solution)/shard_map/psum | solution.py:39
  128.5 1.1 convolution_convert_fusion.1
  129.6 13.4 %all-gather.2 = bf16[128,512]{1,0:T(8,128)(2,1)S(1)} all-gather(bf16[32,512]{1,0:T(8,128)(2,1)S(1)} %convolution_convert_fusion.1), channel_id=4, replica_groups=mesh['groups'=2,'prow'=4,'pcol'=4] {'pcol'}, dimensions={0}, use_global_device_ids=true | all-gather | bytes 163840 | tf_op jit(solution)/shard_map/all_gather | solution.py:43
  143.1 3.9 %conditional.22 = (f32[32,512]{1,0:T(8,128)S(1)}) conditional(s32[]{:T(128)} %convert_element_type.138, () %tuple.90, (s32[4]{0:T(128)S(1)}, bf16[4,32,512]{2,1,0:T(8,128)(2,1)S(1)}, bf16[4,512,512]{2,1,0:T(8,128)(2,1)}) %tuple.136), branch_computations={%region_22.23_spmd, %region_23.24_spmd} | conditional | flops 16777220 | bytes 622646 | solution.py:18
  143.1 0.6 slice.66
  145.6 1.3 fusion.60
  146.9 1.4 conditional.20
  147.1 1.3 fusion.48
  148.3 3.1 %fusion.84 = f32[32,512]{1,0:T(8,128)} fusion(f32[4,32,512]{2,1,0:T(8,128)S(1)} %multiply_add_fusion, f32[32,512]{1,0:T(8,128)S(1)} %get-tuple-element.174, f32[1]{0:T(128)} %slice.182, f32[32,512]{1,0:T(8,128)S(1)} %get-tuple-element.173, f32[1]{0:T(128)} %slice.181, f32[32,512]{1,0:T(8,128)S(1)} %get-tuple-element.172, f32[1]{0:T(128)} %slice.180, ...), kind=kLoop, calls=%fused_computation.92 | loop fusion | flops 131072 | bytes 393232 | tf_op jit(solution)/shard_map/squeeze | solution.py:39
  151.5 0.0 all-reduce.8.cloned.1.call-update
  151.5 29.7 %all-reduce.8.cloned.1.call-done = f32[32,512]{1,0:T(8,128)} async-done(((f32[32,512]{1,0:T(8,128)}), f32[32,512]{1,0:T(8,128)}) %all-reduce.8.cloned.1.call-update) | async-done | bytes 65552 | tf_op jit(solution)/shard_map/psum | solution.py:39
  181.2 1.1 fusion.72
  182.3 0.7 pad_maximum_fusion
  (16 shorter events, 0.2 us)
Async XLA Ops:
  6.5 71.1 %all-reduce.4.cloned.1.call-start = ((), (), s32[]{:S(2)}) async-start(), calls=%async_computation | async-start | bytes 131072 | tf_op jit(solution)/shard_map/psum | solution.py:39
  16.8 60.9 %copy-start = (bf16[4,512,512]{2,1,0:T(8,128)(2,1)S(1)}, bf16[4,512,512]{2,1,0:T(8,128)(2,1)}, u32[]{:S(2)}) copy-start(bf16[4,512,512]{2,1,0:T(8,128)(2,1)} %param.30) | copy-start | bytes 6291460
  16.8 60.9 %copy-start.1 = (bf16[4,32,512]{2,1,0:T(8,128)(2,1)S(1)}, bf16[4,32,512]{2,1,0:T(8,128)(2,1)}, u32[]{:S(2)}) copy-start(bf16[4,32,512]{2,1,0:T(8,128)(2,1)} %param.29) | copy-start | bytes 393220
  38.0 90.5 %all-reduce.6.cloned.1.call-start = ((), (), s32[]{:S(2)}) async-start(), calls=%async_computation.1 | async-start | bytes 131072 | tf_op jit(solution)/shard_map/psum | solution.py:39
  97.0 84.3 %all-reduce.8.cloned.1.call-start = ((), (), s32[]{:S(2)}) async-start(), calls=%async_computation.2 | async-start | bytes 131072 | tf_op jit(solution)/shard_map/psum | solution.py:39
Sparse Core Ops, SparseCore 0:
  38.2 39.4 all-reduce.3
  97.1 31.4 all-reduce.5
  151.6 29.5 all-reduce.7
where the time goes:
time: 192 us; the launch traced here: 190 us
  waiting for transfers between devices  88.5 us (46%)
  blocking collectives  41.9 us (22%)
  between operations  28.1 us (15%)
  matrix products  9.86 us (5%)
  local copies, waits for them, and re-layouts  7.64 us (4%)
  other arithmetic  7.34 us (4%)
  loops' own time  6.09 us (3%)
    psum x3, waiting for transfers between devices, body(): lax.psum(partial_value[level], 'prow')  88.5 us
    all_gather x3, blocking collectives, body(): gathered = lax.all_gather(block[None], 'pcol', axis=0, tiled=True)  41.9 us
    dot_general x8, matrix products, apply_right(): lax.dot_general(left, matrix, (((1,), (1,)), ((), ())), preferred_element...  9.86 us
    another operation x12, loops' own time, spread(): lax.cond(active, lambda slot=slot: apply_right(pick(src_col[slot]), tiles...  6.09 us
  transfers between devices with their start and end apart: 3, of which 3 were waited for; matrix products, arithmetic and copies ran while one was open for 1% of the time, Pallas kernels for 0%

commit v1 on v0

v1 whole, which is shorter than its diff:
```python
import jax
import jax.numpy as jnp
from jax import lax
from jax.experimental import pallas as pl
from jax.experimental.pallas import tpu as pltpu
from jax.sharding import PartitionSpec as P

MESH = pl.DeviceIdType.MESH


def apply_right(left, matrix):
    return lax.dot_general(
        left, matrix, (((1,), (1,)), ((), ())), preferred_element_type=jnp.float32
    )


def kernel(
    cols, rows, source_ref, target_ref, rhs_hbm, dinv_hbm, tiles_hbm, out_ref,
    rhs, dinv, tiles, picked, own, part, xs, local_sem, send_x, recv_x, send_p, recv_p,
):
    levels, slots = rhs.shape[0], tiles.shape[0]
    p, c = lax.axis_index("prow"), lax.axis_index("pcol")

    loads = [pltpu.make_async_copy(rhs_hbm, rhs, local_sem.at[0])]
    for level in range(levels):
        loads.append(
            pltpu.make_async_copy(dinv_hbm.at[level], dinv.at[level], local_sem.at[1 + level])
        )
    tile_load = pltpu.make_async_copy(tiles_hbm, tiles, local_sem.at[1 + levels])
    loads[0].start()
    loads[1].start()
    tile_load.start()
    for load in loads[2:]:
        load.start()

    barrier = pltpu.get_barrier_semaphore()
    for k in range(1, cols):
        pl.semaphore_signal(
            barrier, inc=1, device_id={"pcol": lax.rem(c + k, cols)}, device_id_type=MESH
        )
    for k in range(1, rows):
        pl.semaphore_signal(
            barrier, inc=1, device_id={"prow": lax.rem(p + k, rows)}, device_id_type=MESH
        )

    def send_block(level):
        copies = []
        for k in range(1, cols):
            copy = pltpu.make_async_remote_copy(
                src_ref=own.at[level],
                dst_ref=xs[level].at[c],
                send_sem=send_x.at[level, k],
                recv_sem=recv_x.at[level, k],
                device_id={"pcol": lax.rem(c + k, cols)},
                device_id_type=MESH,
            )
            copy.start()
            copies.append(copy)
        return copies

    def send_part(level):
        copies = []
        for k in range(1, rows):
            copy = pltpu.make_async_remote_copy(
                src_ref=part.at[level, p],
                dst_ref=part.at[level, p],
                send_sem=send_p.at[level, k],
                recv_sem=recv_p.at[level, k],
                device_id={"prow": lax.rem(p + k, rows)},
                device_id_type=MESH,
            )
            copy.start()
            copies.append(copy)
        return copies

    picked[...] = jnp.zeros_like(picked)
    src_level = [source_ref[g] // cols for g in range(slots)]
    src_col = [lax.rem(source_ref[g], cols) for g in range(slots)]
    pending = []
    for level in range(levels):
        if level == 0:
            loads[0].wait()
            short = rhs[0]
        else:
            partial_value = None
            for g in range(slots):
                now = jnp.where(
                    src_level[g] == level - 1, xs[level - 1][src_col[g]], picked[g]
                )
                picked[g] = now
                left = jnp.where(target_ref[g] == level, now, jnp.zeros_like(now))
                term = apply_right(left, tiles[g])
                partial_value = term if partial_value is None else partial_value + term
            part[level - 1, p] = partial_value
            copies = send_part(level - 1)
            for copy in copies:
                copy.wait_recv()
            pending += copies
            total = part[level - 1, 0]
            for q in range(1, rows):
                total = total + part[level - 1, q]
            short = (rhs[level].astype(jnp.float32) - total).astype(jnp.bfloat16)
        loads[1 + level].wait()
        block = apply_right(short, dinv[level]).astype(jnp.bfloat16)
        out_ref[level] = block
        if level + 1 < levels:
            own[level] = block
            xs[level][c] = block
            if level == 0:
                pl.semaphore_wait(barrier, cols + rows - 2)
            copies = send_block(level)
            if level == 0:
                tile_load.wait()
            for copy in copies:
                copy.wait_recv()
            pending += copies
    for copy in pending:
        copy.wait_send()


def solution(mesh):
    rows, cols = mesh.shape["prow"], mesh.shape["pcol"]

    def body(rhs, dinv, tiles, tile_source, tile_target):
        levels, samples, width = rhs.shape
        slots = tiles.shape[0]

        def call(source_ref, target_ref, rhs_hbm, dinv_hbm, tiles_hbm, out_ref,
                 rhs_v, dinv_v, tiles_v, picked, own, part, *rest):
            xs, sems = rest[: levels - 1], rest[levels - 1 :]
            kernel(cols, rows, source_ref, target_ref, rhs_hbm, dinv_hbm, tiles_hbm, out_ref,
                   rhs_v, dinv_v, tiles_v, picked, own, part, xs, *sems)

        return pl.pallas_call(
            call,
            out_shape=jax.ShapeDtypeStruct(rhs.shape, jnp.bfloat16),
            in_specs=[pl.BlockSpec(memory_space=pltpu.SMEM)] * 2
            + [pl.BlockSpec(memory_space=pl.ANY)] * 3,
            out_specs=pl.BlockSpec(memory_space=pltpu.VMEM),
            scratch_shapes=[
                pltpu.VMEM(rhs.shape, jnp.bfloat16),
                pltpu.VMEM(dinv.shape, jnp.bfloat16),
                pltpu.VMEM(tiles.shape, jnp.bfloat16),
                pltpu.VMEM((slots, samples, width), jnp.bfloat16),
                pltpu.VMEM((levels - 1, samples, width), jnp.bfloat16),
                pltpu.VMEM((levels - 1, rows, samples, width), jnp.float32),
            ]
            + [pltpu.VMEM((cols, samples, width), jnp.bfloat16)] * (levels - 1)
            + [
                pltpu.SemaphoreType.DMA((levels + 2,)),
                pltpu.SemaphoreType.DMA((levels - 1, cols)),
                pltpu.SemaphoreType.DMA((levels - 1, cols)),
                pltpu.SemaphoreType.DMA((levels - 1, rows)),
                pltpu.SemaphoreType.DMA((levels - 1, rows)),
            ],
            compiler_params=pltpu.CompilerParams(
                collective_id=0, has_side_effects=True, vmem_limit_bytes=40 * 1024 * 1024
            ),
        )(tile_source, tile_target, rhs, dinv, tiles)

    placed = (
        P("groups", None, "pcol"),
        P("groups", None, "pcol"),
        P(("groups", "prow", "pcol"), None, None),
        P(("groups", "prow", "pcol")),
        P(("groups", "prow", "pcol")),
    )
    return jax.shard_map(
        body, mesh=mesh, in_specs=placed, out_specs=P("groups", None, "pcol"), check_vma=False
    )
```

time: 192 us -> 41.6 us (0.22); the launches traced: 190 us -> 41.3 us
  waiting for transfers between devices: 88.5 us -> 0 us
  blocking collectives: 41.9 us -> 0 us
  Pallas kernels: 0 us -> 35.2 us
  between operations: 28.1 us -> 0.01 us
  matrix products: 9.86 us -> 0 us
  other arithmetic: 7.34 us -> 0 us
  loops' own time: 6.09 us -> 0 us
    psum x3 -> x0, waiting for transfers between devices: 88.5 us -> none  [body(): lax.psum(partial_value[level], 'prow')]
    all_gather x3 -> x0, blocking collectives: 41.9 us -> none  [body(): gathered = lax.all_gather(block[None], 'pcol', axis=0, tiled=True)]
    pallas_call x0 -> x1, Pallas kernels: none -> 35.2 us  [body(): pl.pallas_call(call, out_shape=jax.ShapeDtypeStruct(rhs.shape, jnp.bfloat...]
    dot_general x8 -> x0, matrix products: 9.86 us -> none  [apply_right(): lax.dot_general(left, matrix, (((1,), (1,)), ((), ())), preferred_element...]
    slice x9 -> x0, local copies, waits for them, and re-layouts: 6.28 us -> none  [the longest x4 2.44 us: body(): partial_value[level]]
    another operation x12 -> x0, loops' own time: 6.09 us -> none  [spread(): lax.cond(active, lambda slot=slot: apply_right(pick(src_col[slot]), tiles...]
    unnamed x4 -> x11, local copies, waits for them, and re-layouts: 0.01 us -> 6.05 us
    squeeze x1 -> x0, other arithmetic: 3.15 us -> none  [body(): partial_value[level]]
  transfers between devices with their start and end apart: 3 -> 0, of which waited for: 3 -> 0; matrix products, arithmetic and copies ran while one was open for 1% -> 0% of each run, Pallas kernels for 0% -> 0%
where the time goes in v1:
time: 41.6 us; the launch traced here: 41.3 us
  Pallas kernels  35.2 us (85%)
  local copies, waits for them, and re-layouts  6.05 us (15%)
    pallas_call x1, Pallas kernels, body(): pl.pallas_call(call, out_shape=jax.ShapeDtypeStruct(rhs.shape, jnp.bfloat...  35.2 us
    unnamed x11, local copies, waits for them, and re-layouts  6.05 us

profile of v1, /device:TPU:0, one launch (start us, length us, event | category | flops | bytes accessed | tf_op | source)
XLA Modules:
  0.0 41.3 jit_solution(14241014048814134823)
XLA Ops:
  0.0 0.0 copy-start
  0.0 1.6 %copy-done = bf16[4,512,512]{2,1,0:T(8,128)(2,1)S(1)} copy-done((bf16[4,512,512]{2,1,0:T(8,128)(2,1)S(1)}, bf16[4,512,512]{2,1,0:T(8,128)(2,1)}, u32[]{:S(2)}) %copy-start) | copy-done | bytes 2097176
  1.6 0.0 copy-start.1
  1.6 1.6 %copy-done.1 = bf16[4,512,512]{2,1,0:T(8,128)(2,1)S(1)} copy-done((bf16[4,512,512]{2,1,0:T(8,128)(2,1)S(1)}, bf16[4,512,512]{2,1,0:T(8,128)(2,1)}, u32[]{:S(2)}) %copy-start.1) | copy-done | bytes 2097176
  3.2 0.0 copy-start.2
  3.2 0.9 %copy-done.2 = bf16[4,32,512]{2,1,0:T(8,128)(2,1)S(1)} copy-done((bf16[4,32,512]{2,1,0:T(8,128)(2,1)S(1)}, bf16[4,32,512]{2,1,0:T(8,128)(2,1)}, u32[]{:S(2)}) %copy-start.2) | copy-done | bytes 131096
  4.1 0.0 copy-start.3
  4.1 0.7 %copy-done.3 = s32[4]{0:T(128)S(1)} copy-done((s32[4]{0:T(128)S(1)}, s32[4]{0:T(128)}, u32[]{:S(2)}) %copy-start.3) | copy-done | bytes 40
  4.7 0.0 copy-start.4
  4.7 0.7 %copy-done.4 = s32[4]{0:T(128)S(1)} copy-done((s32[4]{0:T(128)S(1)}, s32[4]{0:T(128)}, u32[]{:S(2)}) %copy-start.4) | copy-done | bytes 40
  5.4 35.2 %shard_map.55 = bf16[4,32,512]{2,1,0:T(8,128)(2,1)S(1)} custom-call(s32[4]{0:T(128)S(1)} %copy-done.3, s32[4]{0:T(128)S(1)} %copy-done.4, bf16[4,32,512]{2,1,0:T(8,128)(2,1)S(1)} %copy-done.2, bf16[4,512,512]{2,1,0:T(8,128)(2,1)S(1)} %copy-done, bf16[4,512,512]{2,1,0:T(8,128)(2,1)S(1)} %copy-done.1), custom_call_target="tpu_custom_call" | custom-call | tf_op jit(solution)/shard_map/pallas_call | solution.py:134
  40.6 0.7 %copy.7 = bf16[4,32,512]{2,1,0:T(8,128)(2,1)} copy(bf16[4,32,512]{2,1,0:T(8,128)(2,1)S(1)} %shard_map.55) | data formatting | bytes 262144
Async XLA Ops:
  0.0 1.6 %copy-start = (bf16[4,512,512]{2,1,0:T(8,128)(2,1)S(1)}, bf16[4,512,512]{2,1,0:T(8,128)(2,1)}, u32[]{:S(2)}) copy-start(bf16[4,512,512]{2,1,0:T(8,128)(2,1)} %dinv_hbm.1) | copy-start | bytes 6291460
  1.6 1.6 %copy-start.1 = (bf16[4,512,512]{2,1,0:T(8,128)(2,1)S(1)}, bf16[4,512,512]{2,1,0:T(8,128)(2,1)}, u32[]{:S(2)}) copy-start(bf16[4,512,512]{2,1,0:T(8,128)(2,1)} %tiles_hbm.1) | copy-start | bytes 6291460
  3.2 0.9 %copy-start.2 = (bf16[4,32,512]{2,1,0:T(8,128)(2,1)S(1)}, bf16[4,32,512]{2,1,0:T(8,128)(2,1)}, u32[]{:S(2)}) copy-start(bf16[4,32,512]{2,1,0:T(8,128)(2,1)} %rhs_hbm.1) | copy-start | bytes 393220
  4.1 0.7 %copy-start.3 = (s32[4]{0:T(128)S(1)}, s32[4]{0:T(128)}, u32[]{:S(2)}) copy-start(s32[4]{0:T(128)} %source_ref.1) | copy-start | bytes 52
  4.7 0.7 %copy-start.4 = (s32[4]{0:T(128)S(1)}, s32[4]{0:T(128)}, u32[]{:S(2)}) copy-start(s32[4]{0:T(128)} %target_ref.1) | copy-start | bytes 52

commit v2 on v0

v2 whole, which is shorter than its diff:
```python
import jax
import jax.numpy as jnp
from jax import lax
from jax.experimental import pallas as pl
from jax.experimental.pallas import tpu as pltpu
from jax.sharding import PartitionSpec as P

MESH = pl.DeviceIdType.MESH
PAIR = 2


def apply_right(left, matrix):
    return lax.dot_general(
        left, matrix, (((1,), (1,)), ((), ())), preferred_element_type=jnp.float32
    )


def kernel(
    cols, rows, source_hbm, target_hbm, rhs_hbm, dinv_hbm, tiles_hbm, out_ref,
    source, target, rhs, dinv, tiles, picked, first, halves, x0, ys, final,
    load_sem, tile_sem, send_tile, recv_tile, send_x0, recv_x0, send_y, recv_y,
    send_half, recv_half, send_final, recv_final,
):
    levels, samples = rhs.shape[0], rhs.shape[1]
    slots = tiles.shape[1]
    half = samples // PAIR
    sums = rows // PAIR
    p, c = lax.axis_index("prow"), lax.axis_index("pcol")
    k, xg = lax.rem(p, PAIR), p // PAIR
    mate = p + 1 - 2 * k
    mine = pl.ds(pl.multiple_of(k * half, half), half)

    def remote(src, dst, send, recv, prow, pcol):
        return pltpu.make_async_remote_copy(
            src_ref=src, dst_ref=dst, send_sem=send, recv_sem=recv,
            device_id={"prow": prow, "pcol": pcol}, device_id_type=MESH,
        )

    peers = []
    for dx in range(sums):
        for dc in range(cols):
            if dx or dc:
                peers.append((lax.rem(xg + dx, sums) * PAIR + k, lax.rem(c + dc, cols), dx, dc))
    column = [lax.rem(p + d, rows) for d in range(1, rows)]

    load_rhs = pltpu.make_async_copy(rhs_hbm, rhs, load_sem.at[0])
    load_dinv = [
        pltpu.make_async_copy(dinv_hbm.at[level], dinv.at[level], load_sem.at[1 + level])
        for level in range(levels)
    ]
    load_source = pltpu.make_async_copy(source_hbm, source.at[0], load_sem.at[1 + levels])
    load_target = pltpu.make_async_copy(target_hbm, target.at[0], load_sem.at[2 + levels])
    load_tile = [
        pltpu.make_async_copy(tiles_hbm.at[g], tiles.at[0, g], tile_sem.at[g])
        for g in range(slots)
    ]
    load_rhs.start()
    load_dinv[0].start()

    barrier = pltpu.get_barrier_semaphore()
    greeted = [(prow, pcol) for prow, pcol, dx, dc in peers]
    for d in range(1, rows):
        if d % PAIR:
            greeted.append((column[d - 1], c))
    for prow, pcol in greeted:
        pl.semaphore_signal(
            barrier, inc=1, device_id={"prow": prow, "pcol": pcol}, device_id_type=MESH
        )
    load_source.start()
    load_target.start()
    for load in load_tile + load_dinv[1:]:
        load.start()

    picked[...] = jnp.zeros_like(picked)
    load_rhs.wait()
    load_dinv[0].wait()
    block = apply_right(rhs[0], dinv[0]).astype(jnp.bfloat16)
    out_ref[0] = block
    first[...] = block
    x0[c] = first[mine]
    pl.semaphore_wait(barrier, len(greeted))

    pending = []
    arrivals = []
    for prow, pcol, dx, dc in peers:
        if dx == 0:
            copy = remote(x0.at[c], x0.at[c], send_x0.at[dc], recv_x0.at[dc], p, pcol)
            copy.start()
            arrivals.append(copy)
    pending += arrivals
    swap = [
        remote(source_hbm, source.at[1], send_tile.at[slots], recv_tile.at[slots], mate, c),
        remote(target_hbm, target.at[1], send_tile.at[slots + 1], recv_tile.at[slots + 1], mate, c),
    ] + [
        remote(tiles_hbm.at[g], tiles.at[1, g], send_tile.at[g], recv_tile.at[g], mate, c)
        for g in range(slots)
    ]
    for copy in swap:
        copy.start()
    pending += swap

    load_source.wait()
    load_target.wait()
    swap[0].wait_recv()
    swap[1].wait_recv()
    slot = [(j, g) for j in range(PAIR) for g in range(slots)]
    src_level = {s: source[s[0], s[1]] // cols for s in slot}
    src_col = {s: lax.rem(source[s[0], s[1]], cols) for s in slot}
    to_level = {s: target[s[0], s[1]] for s in slot}

    half_copies = []
    for level in range(1, levels):
        for copy in arrivals:
            copy.wait_recv()
        partial_value = None
        for s in slot:
            if level == 1:
                load_tile[s[1]].wait() if s[0] == 0 else swap[2 + s[1]].wait_recv()
                seen = x0[src_col[s]]
            else:
                seen = ys[level - 2][0, src_col[s]].astype(jnp.float32)
                for q in range(1, sums):
                    seen = seen + ys[level - 2][q, src_col[s]].astype(jnp.float32)
                seen = seen.astype(jnp.bfloat16)
            now = jnp.where(src_level[s] == level - 1, seen, picked[s])
            picked[s] = now
            left = jnp.where(to_level[s] == level, now, jnp.zeros_like(now))
            term = apply_right(left, tiles[s])
            partial_value = term if partial_value is None else partial_value + term
        if level + 1 < levels:
            begin = jnp.where(xg == 0, rhs[level, mine].astype(jnp.float32), 0.0)
            short = begin - partial_value
            high = short.astype(jnp.bfloat16)
            low = (short - high.astype(jnp.float32)).astype(jnp.bfloat16)
            load_dinv[level].wait()
            both = apply_right(jnp.concatenate([high, low], axis=0), dinv[level])
            y = ys[level - 1]
            y[xg, c] = (both[:half] + both[half:]).astype(jnp.bfloat16)
            arrivals = []
            for prow, pcol, dx, dc in peers:
                copy = remote(
                    y.at[xg, c], y.at[xg, c],
                    send_y.at[level - 1, dx, dc], recv_y.at[level - 1, dx, dc], prow, pcol,
                )
                copy.start()
                arrivals.append(copy)
            pending += arrivals
        else:
            final[p] = partial_value
            arrivals = []
            for d in range(1, rows):
                copy = remote(
                    final.at[p], final.at[p], send_final.at[d], recv_final.at[d], column[d - 1], c
                )
                copy.start()
                arrivals.append(copy)
            pending += arrivals
        if level >= 2:
            y = ys[level - 2]
            total = y[0, c].astype(jnp.float32)
            for q in range(1, sums):
                total = total + y[q, c].astype(jnp.float32)
            halves[level - 2, k] = total.astype(jnp.bfloat16)
            copy = remote(
                halves.at[level - 2, k], halves.at[level - 2, k],
                send_half.at[level - 2], recv_half.at[level - 2], mate, c,
            )
            copy.start()
            half_copies.append(copy)
    for level, copy in enumerate(half_copies):
        copy.wait_recv()
        for j in range(PAIR):
            out_ref[1 + level, j * half : (j + 1) * half] = halves[level, j]
    pending += half_copies
    load_dinv[levels - 1].wait()
    for copy in arrivals:
        copy.wait_recv()
    shorts = []
    for j in range(PAIR):
        total = final[j]
        for q in range(1, sums):
            total = total + final[q * PAIR + j]
        begin = rhs[levels - 1, j * half : (j + 1) * half].astype(jnp.float32)
        shorts.append((begin - total).astype(jnp.bfloat16))
    short = jnp.concatenate(shorts, axis=0)
    out_ref[levels - 1] = apply_right(short, dinv[levels - 1]).astype(jnp.bfloat16)
    for copy in pending:
        copy.wait_send()


def solution(mesh):
    rows, cols = mesh.shape["prow"], mesh.shape["pcol"]

    def body(rhs, dinv, tiles, tile_source, tile_target):
        levels, samples, width = rhs.shape
        slots = tiles.shape[0]
        half, sums = samples // PAIR, rows // PAIR

        def call(*refs):
            ins, scratch, rest = refs[:6], refs[6:15], refs[15:]
            ys, rest = rest[: levels - 2], rest[levels - 2 :]
            kernel(cols, rows, *ins, *scratch, ys, *rest)

        dma = pltpu.SemaphoreType.DMA
        return pl.pallas_call(
            call,
            out_shape=jax.ShapeDtypeStruct(rhs.shape, jnp.bfloat16),
            in_specs=[pl.BlockSpec(memory_space=pl.ANY)] * 5,
            out_specs=pl.BlockSpec(memory_space=pltpu.VMEM),
            scratch_shapes=[
                pltpu.SMEM((PAIR, slots), jnp.int32),
                pltpu.SMEM((PAIR, slots), jnp.int32),
                pltpu.VMEM(rhs.shape, jnp.bfloat16),
                pltpu.VMEM(dinv.shape, jnp.bfloat16),
                pltpu.VMEM((PAIR,) + tiles.shape, jnp.bfloat16),
                pltpu.VMEM((PAIR, slots, half, width), jnp.bfloat16),
                pltpu.VMEM((samples, width), jnp.bfloat16),
                pltpu.VMEM((levels - 2, PAIR, half, width), jnp.bfloat16),
                pltpu.VMEM((cols, half, width), jnp.bfloat16),
            ]
            + [pltpu.VMEM((sums, cols, half, width), jnp.bfloat16)] * (levels - 2)
            + [
                pltpu.VMEM((rows, half, width), jnp.float32),
                dma((levels + 3,)),
                dma((slots,)),
                dma((slots + 2,)),
                dma((slots + 2,)),
                dma((cols,)),
                dma((cols,)),
                dma((levels - 2, sums, cols)),
                dma((levels - 2, sums, cols)),
                dma((levels - 2,)),
                dma((levels - 2,)),
                dma((rows,)),
                dma((rows,)),
            ],
            compiler_params=pltpu.CompilerParams(
                collective_id=0, has_side_effects=True, vmem_limit_bytes=60 * 1024 * 1024
            ),
        )(tile_source, tile_target, rhs, dinv, tiles)

    placed = (
        P("groups", None, "pcol"),
        P("groups", None, "pcol"),
        P(("groups", "prow", "pcol"), None, None),
        P(("groups", "prow", "pcol")),
        P(("groups", "prow", "pcol")),
    )
    return jax.shard_map(
        body, mesh=mesh, in_specs=placed, out_specs=P("groups", None, "pcol"), check_vma=False
    )
```

time: 192 us -> 29.3 us (0.15); the launches traced: 190 us -> 29.1 us
  waiting for transfers between devices: 88.5 us -> 0 us
  blocking collectives: 41.9 us -> 0 us
  between operations: 28.1 us -> 0.01 us
  Pallas kernels: 0 us -> 27.5 us
  matrix products: 9.86 us -> 0 us
  other arithmetic: 7.34 us -> 0 us
  loops' own time: 6.09 us -> 0 us
  local copies, waits for them, and re-layouts: 7.64 us -> 1.57 us
    psum x3 -> x0, waiting for transfers between devices: 88.5 us -> none  [body(): lax.psum(partial_value[level], 'prow')]
    all_gather x3 -> x0, blocking collectives: 41.9 us -> none  [body(): gathered = lax.all_gather(block[None], 'pcol', axis=0, tiled=True)]
    pallas_call x0 -> x1, Pallas kernels: none -> 27.5 us  [body(): pl.pallas_call(call, out_shape=jax.ShapeDtypeStruct(rhs.shape, jnp.bfloat...]
    dot_general x8 -> x0, matrix products: 9.86 us -> none  [apply_right(): lax.dot_general(left, matrix, (((1,), (1,)), ((), ())), preferred_element...]
    slice x9 -> x0, local copies, waits for them, and re-layouts: 6.28 us -> none  [the longest x4 2.44 us: body(): partial_value[level]]
    another operation x12 -> x0, loops' own time: 6.09 us -> none  [spread(): lax.cond(active, lambda slot=slot: apply_right(pick(src_col[slot]), tiles...]
    squeeze x1 -> x0, other arithmetic: 3.15 us -> none  [body(): partial_value[level]]
    convert_element_type x2 -> x0, other arithmetic: 2.48 us -> none  [spread(): (jnp.arange(levels, dtype=jnp.int32) == tile_target[slot]).astype(jnp.flo...]
  transfers between devices with their start and end apart: 3 -> 0, of which waited for: 3 -> 0; matrix products, arithmetic and copies ran while one was open for 1% -> 0% of each run, Pallas kernels for 0% -> 0%
where the time goes in v2:
time: 29.3 us; the launch traced here: 29.1 us
  Pallas kernels  27.5 us (94%)
  local copies, waits for them, and re-layouts  1.57 us (5%)
    pallas_call x1, Pallas kernels, body(): pl.pallas_call(call, out_shape=jax.ShapeDtypeStruct(rhs.shape, jnp.bfloat...  27.5 us
    unnamed x1, local copies, waits for them, and re-layouts  1.57 us

profile of v2, /device:TPU:0, one launch (start us, length us, event | category | flops | bytes accessed | tf_op | source)
XLA Modules:
  0.0 29.1 jit_solution(14003688470504718852)
XLA Ops:
  0.0 27.5 %shard_map.55 = bf16[4,32,512]{2,1,0:T(8,128)(2,1)} custom-call(s32[4]{0:T(128)} %refs_0_.1, s32[4]{0:T(128)} %refs_1_.1, bf16[4,32,512]{2,1,0:T(8,128)(2,1)} %refs_2_.1, bf16[4,512,512]{2,1,0:T(8,128)(2,1)} %refs_3_.1, bf16[4,512,512]{2,1,0:T(8,128)(2,1)} %refs_4_.1), custom_call_target="tpu_custom_call" | custom-call | tf_op jit(solution)/shard_map/pallas_call | solution.py:205
  27.5 1.6 %copy.7 = bf16[4,32,512]{2,1,0:T(8,128)(2,1)} copy(bf16[4,32,512]{2,1,0:T(8,128)(2,1)} %shard_map.55) | data formatting | bytes 262144

commit v3 on v2

--- a/solution.py
+++ b/solution.py
@@ -15,14 +15,18 @@
     )
 
 
+def apply_plain(left, matrix):
+    return jnp.dot(left, matrix, preferred_element_type=jnp.float32)
+
+
 def kernel(
     cols, rows, source_hbm, target_hbm, rhs_hbm, dinv_hbm, tiles_hbm, out_ref,
-    source, target, rhs, dinv, tiles, picked, first, halves, x0, ys, final,
+    source, target, rhs, dinv, raw, tiles, picked, first, halves, x0, ys, final,
     load_sem, tile_sem, send_tile, recv_tile, send_x0, recv_x0, send_y, recv_y,
-    send_half, recv_half, send_final, recv_final,
+    send_half, recv_half, send_final, recv_final, vouch,
 ):
     levels, samples = rhs.shape[0], rhs.shape[1]
-    slots = tiles.shape[1]
+    slots = raw.shape[0]
     half = samples // PAIR
     sums = rows // PAIR
     p, c = lax.axis_index("prow"), lax.axis_index("pcol")
@@ -41,6 +45,7 @@
         for dc in range(cols):
             if dx or dc:
                 peers.append((lax.rem(xg + dx, sums) * PAIR + k, lax.rem(c + dc, cols), dx, dc))
+    peers = peers[::-1]
     column = [lax.rem(p + d, rows) for d in range(1, rows)]
 
     load_rhs = pltpu.make_async_copy(rhs_hbm, rhs, load_sem.at[0])
@@ -51,17 +56,15 @@
     load_source = pltpu.make_async_copy(source_hbm, source.at[0], load_sem.at[1 + levels])
     load_target = pltpu.make_async_copy(target_hbm, target.at[0], load_sem.at[2 + levels])
     load_tile = [
-        pltpu.make_async_copy(tiles_hbm.at[g], tiles.at[0, g], tile_sem.at[g])
+        pltpu.make_async_copy(tiles_hbm.at[g], raw.at[g], tile_sem.at[g])
         for g in range(slots)
     ]
     load_rhs.start()
     load_dinv[0].start()
 
     barrier = pltpu.get_barrier_semaphore()
-    greeted = [(prow, pcol) for prow, pcol, dx, dc in peers]
-    for d in range(1, rows):
-        if d % PAIR:
-            greeted.append((column[d - 1], c))
+    greeted = [(prow, pcol) for prow, pcol, dx, dc in peers if dx == 0]
+    greeted += [(prow, c) for prow in column]
     for prow, pcol in greeted:
         pl.semaphore_signal(
             barrier, inc=1, device_id={"prow": prow, "pcol": pcol}, device_id_type=MESH
@@ -78,6 +81,9 @@
     out_ref[0] = block
     first[...] = block
     x0[c] = first[mine]
+    for g in range(slots):
+        load_tile[g].wait()
+        tiles[0, g] = raw[g].T
     pl.semaphore_wait(barrier, len(greeted))
 
     pending = []
@@ -92,13 +98,21 @@
         remote(source_hbm, source.at[1], send_tile.at[slots], recv_tile.at[slots], mate, c),
         remote(target_hbm, target.at[1], send_tile.at[slots + 1], recv_tile.at[slots + 1], mate, c),
     ] + [
-        remote(tiles_hbm.at[g], tiles.at[1, g], send_tile.at[g], recv_tile.at[g], mate, c)
+        remote(tiles.at[0, g], tiles.at[1, g], send_tile.at[g], recv_tile.at[g], mate, c)
         for g in range(slots)
     ]
     for copy in swap:
         copy.start()
+    for prow, pcol, dx, dc in peers:
+        if dx and dc == 0:
+            pl.semaphore_signal(
+                vouch, inc=1, device_id={"prow": prow, "pcol": pcol}, device_id_type=MESH
+            )
     pending += swap
 
+    for level in range(1, levels):
+        load_dinv[level].wait()
+        dinv[level] = dinv[level].T
     load_source.wait()
     load_target.wait()
     swap[0].wait_recv()
@@ -115,7 +129,8 @@
         partial_value = None
         for s in slot:
             if level == 1:
-                load_tile[s[1]].wait() if s[0] == 0 else swap[2 + s[1]].wait_recv()
+                if s[0] == 1:
+                    swap[2 + s[1]].wait_recv()
                 seen = x0[src_col[s]]
             else:
                 seen = ys[level - 2][0, src_col[s]].astype(jnp.float32)
@@ -125,15 +140,16 @@
             now = jnp.where(src_level[s] == level - 1, seen, picked[s])
             picked[s] = now
             left = jnp.where(to_level[s] == level, now, jnp.zeros_like(now))
-            term = apply_right(left, tiles[s])
+            term = apply_plain(left, tiles[s])
             partial_value = term if partial_value is None else partial_value + term
         if level + 1 < levels:
             begin = jnp.where(xg == 0, rhs[level, mine].astype(jnp.float32), 0.0)
             short = begin - partial_value
             high = short.astype(jnp.bfloat16)
             low = (short - high.astype(jnp.float32)).astype(jnp.bfloat16)
-            load_dinv[level].wait()
-            both = apply_right(jnp.concatenate([high, low], axis=0), dinv[level])
+            both = apply_plain(jnp.concatenate([high, low], axis=0), dinv[level])
+            if level == 1:
+                pl.semaphore_wait(vouch, sums - 1)
             y = ys[level - 1]
             y[xg, c] = (both[:half] + both[half:]).astype(jnp.bfloat16)
             arrivals = []
@@ -172,7 +188,6 @@
         for j in range(PAIR):
             out_ref[1 + level, j * half : (j + 1) * half] = halves[level, j]
     pending += half_copies
-    load_dinv[levels - 1].wait()
     for copy in arrivals:
         copy.wait_recv()
     shorts = []
@@ -183,7 +198,7 @@
         begin = rhs[levels - 1, j * half : (j + 1) * half].astype(jnp.float32)
         shorts.append((begin - total).astype(jnp.bfloat16))
     short = jnp.concatenate(shorts, axis=0)
-    out_ref[levels - 1] = apply_right(short, dinv[levels - 1]).astype(jnp.bfloat16)
+    out_ref[levels - 1] = apply_plain(short, dinv[levels - 1]).astype(jnp.bfloat16)
     for copy in pending:
         copy.wait_send()
 
@@ -197,7 +212,7 @@
         half, sums = samples // PAIR, rows // PAIR
 
         def call(*refs):
-            ins, scratch, rest = refs[:6], refs[6:15], refs[15:]
+            ins, scratch, rest = refs[:6], refs[6:16], refs[16:]
             ys, rest = rest[: levels - 2], rest[levels - 2 :]
             kernel(cols, rows, *ins, *scratch, ys, *rest)
 
@@ -212,6 +227,7 @@
                 pltpu.SMEM((PAIR, slots), jnp.int32),
                 pltpu.VMEM(rhs.shape, jnp.bfloat16),
                 pltpu.VMEM(dinv.shape, jnp.bfloat16),
+                pltpu.VMEM(tiles.shape, jnp.bfloat16),
                 pltpu.VMEM((PAIR,) + tiles.shape, jnp.bfloat16),
                 pltpu.VMEM((PAIR, slots, half, width), jnp.bfloat16),
                 pltpu.VMEM((samples, width), jnp.bfloat16),
@@ -233,6 +249,7 @@
                 dma((levels - 2,)),
                 dma((rows,)),
                 dma((rows,)),
+                pltpu.SemaphoreType.REGULAR,
             ],
             compiler_params=pltpu.CompilerParams(
                 collective_id=0, has_side_effects=True, vmem_limit_bytes=60 * 1024 * 1024

time: 29.3 us -> 27 us (0.922)
  Pallas kernels: 27.5 us -> 25.3 us
    pallas_call x1, Pallas kernels: 27.5 us -> 25.3 us  [body(): pl.pallas_call(call, out_shape=jax.ShapeDtypeStruct(rhs.shape, jnp.bfloat...]
where the time goes in v3:
time: 27 us; the launch traced here: 26.9 us
  Pallas kernels  25.3 us (94%)
  local copies, waits for them, and re-layouts  1.57 us (6%)
    pallas_call x1, Pallas kernels, body(): pl.pallas_call(call, out_shape=jax.ShapeDtypeStruct(rhs.shape, jnp.bfloat...  25.3 us
    unnamed x1, local copies, waits for them, and re-layouts  1.57 us

profile of v3, /device:TPU:0, one launch (start us, length us, event | category | flops | bytes accessed | tf_op | source)
XLA Modules:
  0.0 26.9 jit_solution(2455273950710658684)
XLA Ops:
  0.0 25.3 %shard_map.55 = bf16[4,32,512]{2,1,0:T(8,128)(2,1)} custom-call(s32[4]{0:T(128)} %refs_0_.1, s32[4]{0:T(128)} %refs_1_.1, bf16[4,32,512]{2,1,0:T(8,128)(2,1)} %refs_2_.1, bf16[4,512,512]{2,1,0:T(8,128)(2,1)} %refs_3_.1, bf16[4,512,512]{2,1,0:T(8,128)(2,1)} %refs_4_.1), custom_call_target="tpu_custom_call" | custom-call | tf_op jit(solution)/shard_map/pallas_call | solution.py:220
  25.3 1.6 %copy.7 = bf16[4,32,512]{2,1,0:T(8,128)(2,1)} copy(bf16[4,32,512]{2,1,0:T(8,128)(2,1)} %shard_map.55) | data formatting | bytes 262144

commit v4 on v3

--- a/solution.py
+++ b/solution.py
@@ -20,8 +20,8 @@
 
 
 def kernel(
-    cols, rows, source_hbm, target_hbm, rhs_hbm, dinv_hbm, tiles_hbm, out_ref,
-    source, target, rhs, dinv, raw, tiles, picked, first, halves, x0, ys, final,
+    cols, rows, source_hbm, target_hbm, rhs_hbm, dinv_hbm, tiles_hbm, out_hbm,
+    out_ref, store_sem, source, target, rhs, dinv, raw, tiles, picked, first, halves, x0, ys, final,
     load_sem, tile_sem, send_tile, recv_tile, send_x0, recv_x0, send_y, recv_y,
     send_half, recv_half, send_final, recv_final, vouch,
 ):
@@ -40,12 +40,17 @@
             device_id={"prow": prow, "pcol": pcol}, device_id_type=MESH,
         )
 
+    side = lax.div(c, (cols + 1) // 2)
+    others = []
+    for t in range(cols - 1):
+        down, up = cols - 1 - t, t
+        down = down - lax.div(c - down + cols, cols)
+        up = up + lax.div(up - c + cols, cols)
+        others.append((t + 1, down + side * (up - down)))
     peers = []
-    for dx in range(sums):
-        for dc in range(cols):
-            if dx or dc:
-                peers.append((lax.rem(xg + dx, sums) * PAIR + k, lax.rem(c + dc, cols), dx, dc))
-    peers = peers[::-1]
+    for t, pcol in others + [(0, c)]:
+        for dx in range(sums - 1, -(t > 0), -1):
+            peers.append((lax.rem(xg + dx, sums) * PAIR + k, pcol, dx, t))
     column = [lax.rem(p + d, rows) for d in range(1, rows)]
 
     load_rhs = pltpu.make_async_copy(rhs_hbm, rhs, load_sem.at[0])
@@ -90,10 +95,12 @@
     arrivals = []
     for prow, pcol, dx, dc in peers:
         if dx == 0:
-            copy = remote(x0.at[c], x0.at[c], send_x0.at[dc], recv_x0.at[dc], p, pcol)
+            copy = remote(x0.at[c], x0.at[c], send_x0.at[dc], recv_x0.at[c], p, pcol)
             copy.start()
-            arrivals.append(copy)
-    pending += arrivals
+            pending.append(copy)
+            arrivals.append(
+                remote(x0.at[pcol], x0.at[pcol], send_x0.at[dc], recv_x0.at[pcol], p, pcol)
+            )
     swap = [
         remote(source_hbm, source.at[1], send_tile.at[slots], recv_tile.at[slots], mate, c),
         remote(target_hbm, target.at[1], send_tile.at[slots + 1], recv_tile.at[slots + 1], mate, c),
@@ -156,11 +163,17 @@
             for prow, pcol, dx, dc in peers:
                 copy = remote(
                     y.at[xg, c], y.at[xg, c],
-                    send_y.at[level - 1, dx, dc], recv_y.at[level - 1, dx, dc], prow, pcol,
+                    send_y.at[level - 1, dx, dc], recv_y.at[level - 1, xg, c], prow, pcol,
                 )
                 copy.start()
-                arrivals.append(copy)
-            pending += arrivals
+                pending.append(copy)
+                q = lax.rem(xg + dx, sums)
+                arrivals.append(
+                    remote(
+                        y.at[q, pcol], y.at[q, pcol],
+                        send_y.at[level - 1, dx, dc], recv_y.at[level - 1, q, pcol], prow, pcol,
+                    )
+                )
         else:
             final[p] = partial_value
             arrivals = []
@@ -187,6 +200,10 @@
         copy.wait_recv()
         for j in range(PAIR):
             out_ref[1 + level, j * half : (j + 1) * half] = halves[level, j]
+    early = pltpu.make_async_copy(
+        out_ref.at[: levels - 1], out_hbm.at[: levels - 1], store_sem.at[0]
+    )
+    early.start()
     pending += half_copies
     for copy in arrivals:
         copy.wait_recv()
@@ -199,8 +216,12 @@
         shorts.append((begin - total).astype(jnp.bfloat16))
     short = jnp.concatenate(shorts, axis=0)
     out_ref[levels - 1] = apply_plain(short, dinv[levels - 1]).astype(jnp.bfloat16)
+    last = pltpu.make_async_copy(out_ref.at[levels - 1], out_hbm.at[levels - 1], store_sem.at[1])
+    last.start()
     for copy in pending:
         copy.wait_send()
+    early.wait()
+    last.wait()
 
 
 def solution(mesh):
@@ -212,7 +233,7 @@
         half, sums = samples // PAIR, rows // PAIR
 
         def call(*refs):
-            ins, scratch, rest = refs[:6], refs[6:16], refs[16:]
+            ins, scratch, rest = refs[:6], refs[6:18], refs[18:]
             ys, rest = rest[: levels - 2], rest[levels - 2 :]
             kernel(cols, rows, *ins, *scratch, ys, *rest)
 
@@ -221,8 +242,10 @@
             call,
             out_shape=jax.ShapeDtypeStruct(rhs.shape, jnp.bfloat16),
             in_specs=[pl.BlockSpec(memory_space=pl.ANY)] * 5,
-            out_specs=pl.BlockSpec(memory_space=pltpu.VMEM),
+            out_specs=pl.BlockSpec(memory_space=pl.ANY),
             scratch_shapes=[
+                pltpu.VMEM(rhs.shape, jnp.bfloat16),
+                dma((2,)),
                 pltpu.SMEM((PAIR, slots), jnp.int32),
                 pltpu.SMEM((PAIR, slots), jnp.int32),
                 pltpu.VMEM(rhs.shape, jnp.bfloat16),

time: 27 us -> 26.3 us (0.974)
  Pallas kernels: 25.3 us -> 24.5 us
    pallas_call x1, Pallas kernels: 25.3 us -> 24.5 us  [body(): pl.pallas_call(call, out_shape=jax.ShapeDtypeStruct(rhs.shape, jnp.bfloat...]
where the time goes in v4:
time: 26.3 us; the launch traced here: 26.1 us
  Pallas kernels  24.5 us (93%)
  local copies, waits for them, and re-layouts  1.57 us (6%)
    pallas_call x1, Pallas kernels, body(): pl.pallas_call(call, out_shape=jax.ShapeDtypeStruct(rhs.shape, jnp.bfloat...  24.5 us
    unnamed x1, local copies, waits for them, and re-layouts  1.57 us

profile of v4, /device:TPU:0, one launch (start us, length us, event | category | flops | bytes accessed | tf_op | source)
XLA Modules:
  0.0 26.1 jit_solution(2668078040162571711)
XLA Ops:
  0.0 24.5 %shard_map.55 = bf16[4,32,512]{2,1,0:T(8,128)(2,1)} custom-call(s32[4]{0:T(128)} %refs_0_.1, s32[4]{0:T(128)} %refs_1_.1, bf16[4,32,512]{2,1,0:T(8,128)(2,1)} %refs_2_.1, bf16[4,512,512]{2,1,0:T(8,128)(2,1)} %refs_3_.1, bf16[4,512,512]{2,1,0:T(8,128)(2,1)} %refs_4_.1), custom_call_target="tpu_custom_call" | custom-call | tf_op jit(solution)/shard_map/pallas_call | solution.py:241
  24.6 1.6 %copy.7 = bf16[4,32,512]{2,1,0:T(8,128)(2,1)} copy(bf16[4,32,512]{2,1,0:T(8,128)(2,1)} %shard_map.55) | data formatting | bytes 262144
